TPU v7x, 32 devices: a whole 2x2x4 slice. The times are simulated.
32 devices in a mesh: groups: 2 (over y), rows: 16 (over z, x, core).
Axes of the slice: x: 2, y: 2, z: 4, core: 2. Of those that a mesh axis runs over, the one named last changes fastest.
Arguments:
- snapshots: bfloat16 [32768, 4096], P(('groups', 'rows')), parts along dimension 0, may hold values from -100 to 100
- test_matrix: bfloat16 [4096, 80], replicated, may hold values from -6 to 6
Outputs:
- basis: float32 [32768, 80], P(('groups', 'rows')), parts along dimension 0
- coefficients: float32 [8192, 80], P(('groups', 'rows')), parts along dimension 0
There are 2 independent parts, one for each index of `groups`. A program takes and returns all parts, laid end to end along the dimension named above; an argument that names none is the same for every part. Nothing has to cross between parts.
All inputs are finite; a program needn't handle non-finite values.
Results may differ from a plain program's by a relative error of at most 0.0039.
Values may be sent and summed in bfloat16 or wider, within the bound.
A program may use at most 64 MiB of HBM per device.

v0:
```python
import math

import jax
import jax.numpy as jnp
from jax import lax
from jax.sharding import PartitionSpec as P


def orthonormalize(sketch):
    local_gram = jnp.dot(sketch.T, sketch, precision=lax.Precision.HIGHEST)
    gram_matrix = lax.psum(local_gram, "rows")
    factor = jnp.linalg.cholesky(gram_matrix)
    return lax.linalg.triangular_solve(
        factor, sketch, left_side=False, lower=True, transpose_a=True
    )


def transpose_product(snapshots, half_basis):
    return lax.dot_general(
        snapshots, half_basis, (((0,), (0,)), ((), ())), preferred_element_type=jnp.float32
    )


def make_projector(snapshots, half_basis):
    return transpose_product(snapshots, half_basis)


def shards(snapshots, test_matrix):
    devices = lax.axis_size("rows")
    sketch = jnp.dot(snapshots, test_matrix, preferred_element_type=jnp.float32)
    first_basis = orthonormalize(sketch)
    first_half = first_basis.astype(jnp.bfloat16)
    projection = lax.psum(transpose_product(snapshots, first_half), "rows")
    power = jnp.dot(snapshots, projection.astype(jnp.bfloat16), preferred_element_type=jnp.float32)
    final_basis = orthonormalize(orthonormalize(power))
    final_half = final_basis.astype(jnp.bfloat16)
    coefficients = lax.psum_scatter(
        make_projector(snapshots, final_half), "rows", scatter_dimension=0, tiled=True
    )
    basis = final_basis * math.sqrt(snapshots.shape[0] * devices)
    return (basis, coefficients)


def solution(mesh):
    in_specs = (P(("groups", "rows"), None), P())
    out_specs = (P(("groups", "rows"), None), P(("groups", "rows"), None))
    return jax.shard_map(shards, mesh=mesh, in_specs=in_specs, out_specs=out_specs, check_vma=False)
```

profile of v0, /device:TPU:0, one launch (start us, length us, event | category | flops | bytes accessed | tf_op | source)
XLA Modules:
  0.0 390.3 jit_solution(8512224228099008964)
XLA Ops:
  7.2 0.0 reduce-scatter.2.cloned.1.call-start
  7.2 1.0 copy-done
  8.3 6.0 %fusion.18 = f32[1024,80]{0,1:T(8,128)S(1)} fusion(bf16[1024,4096]{1,0:T(8,128)(2,1)} %param.5, bf16[4096,80]{0,1:T(8,128)(2,1)S(1)} %copy-done), kind=kOutput, calls=%fused_computation.36 | convolution fusion | flops 671088640 | bytes 9371648 | tf_op jit(solution)/shard_map/dot_general | solution.py:30
  14.3 0.4 fusion.19
  14.7 63.0 %psum.28 = f32[80,80]{0,1:T(8,128)S(1)} all-reduce(f32[80,80]{0,1:T(8,128)S(1)} %fusion.19), channel_id=1, replica_groups=mesh['groups'=2,'rows'=16] {'rows'}, use_global_device_ids=true, to_apply=%region_0.0 | all-reduce | flops 6400 | bytes 51200 | tf_op jit(solution)/shard_map/psum | solution.py:11
  77.7 0.1 copy.5
  77.8 7.3 %cholesky.59 = f32[80,80]{1,0:T(8,128)S(1)} custom-call(f32[80,80]{1,0:T(8,128)S(1)} %fusion.13), custom_call_target="Cholesky" | custom-call | tf_op jit(solution)/shard_map/jit(cholesky)/cholesky | solution.py:12
  85.2 0.6 compare_reduce_fusion.2
  85.8 0.7 fusion.5
  86.5 6.1 %custom-call.7 = f32[1,80,80]{1,2,0:T(8,128)S(1)} custom-call(f32[1,80,80]{2,1,0:T(8,128)S(1)} %fusion.5), custom_call_target="InvertDiagBlocksLowerTriangular" | custom-call | tf_op jit(solution)/shard_map/triangular_solve/custom-call.0 | solution.py:13
  92.6 0.5 fusion
  93.1 4.9 %convolution_bitcast_fusion.1 = f32[4096,80]{0,1:T(8,128)S(1)} fusion(bf16[1024,80]{0,1:T(8,128)(2,1)S(1)} %fusion, bf16[1024,4096]{1,0:T(8,128)(2,1)} %param.5), kind=kOutput, calls=%fused_computation.1 | convolution fusion | flops 671088640 | bytes 9863168 | tf_op jit(solution)/shard_map/dot_general | solution.py:19
  98.0 69.6 %all-reduce.1 = bf16[4096,80]{0,1:T(8,128)(2,1)S(1)} all-reduce(f32[4096,80]{0,1:T(8,128)S(1)} %convolution_bitcast_fusion.1), channel_id=1, replica_groups=mesh['groups'=2,'rows'=16] {'rows'}, use_global_device_ids=true, to_apply=%region_3.6 | all-reduce | flops 327680 | bytes 1966080 | tf_op jit(solution)/shard_map/psum | solution.py:33
  167.6 6.0 %fusion.22 = f32[80,1024]{1,0:T(8,128)S(1)} fusion(bf16[4096,80]{0,1:T(8,128)(2,1)S(1)} %all-reduce.1, bf16[1024,4096]{1,0:T(8,128)(2,1)} %param.5), kind=kOutput, calls=%fused_computation.40 | convolution fusion | flops 671088640 | bytes 9371648 | tf_op jit(solution)/shard_map/dot_general | solution.py:34
  173.6 0.4 fusion.20
  174.1 57.9 %psum.30 = f32[80,80]{0,1:T(8,128)S(1)} all-reduce(f32[80,80]{0,1:T(8,128)S(1)} %fusion.20), channel_id=1, replica_groups=mesh['groups'=2,'rows'=16] {'rows'}, use_global_device_ids=true, to_apply=%region_4.7 | all-reduce | flops 6400 | bytes 51200 | tf_op jit(solution)/shard_map/psum | solution.py:11
  231.9 0.1 copy.7
  232.0 7.3 %cholesky.70 = f32[80,80]{1,0:T(8,128)S(1)} custom-call(f32[80,80]{1,0:T(8,128)S(1)} %fusion.11), custom_call_target="Cholesky" | custom-call | tf_op jit(solution)/shard_map/jit(cholesky)/cholesky | solution.py:12
  239.4 0.6 compare_reduce_fusion.1
  240.0 0.7 fusion.6
  240.7 6.1 %custom-call.8 = f32[1,80,80]{1,2,0:T(8,128)S(1)} custom-call(f32[1,80,80]{2,1,0:T(8,128)S(1)} %fusion.6), custom_call_target="InvertDiagBlocksLowerTriangular" | custom-call | tf_op jit(solution)/shard_map/triangular_solve/custom-call.0 | solution.py:13
  246.8 0.5 convolution_bitcast_fusion.3
  247.3 0.4 fusion.21
  247.7 57.7 %psum.31 = f32[80,80]{0,1:T(8,128)S(1)} all-reduce(f32[80,80]{0,1:T(8,128)S(1)} %fusion.21), channel_id=1, replica_groups=mesh['groups'=2,'rows'=16] {'rows'}, use_global_device_ids=true, to_apply=%region_5.8 | all-reduce | flops 6400 | bytes 51200 | tf_op jit(solution)/shard_map/psum | solution.py:11
  305.4 0.1 copy.9
  305.5 7.3 %cholesky.81 = f32[80,80]{1,0:T(8,128)S(1)} custom-call(f32[80,80]{1,0:T(8,128)S(1)} %fusion.9), custom_call_target="Cholesky" | custom-call | tf_op jit(solution)/shard_map/jit(cholesky)/cholesky | solution.py:12
  312.9 0.6 compare_reduce_fusion
  313.5 0.7 fusion.7
  314.2 6.1 %custom-call.9 = f32[1,80,80]{1,2,0:T(8,128)S(1)} custom-call(f32[1,80,80]{2,1,0:T(8,128)S(1)} %fusion.7), custom_call_target="InvertDiagBlocksLowerTriangular" | custom-call | tf_op jit(solution)/shard_map/triangular_solve/custom-call.0 | solution.py:13
  320.3 1.2 broadcast_multiply_fusion
  321.5 6.0 %convolution_bitcast_fusion = f32[4096,80]{0,1:T(8,128)} fusion(bf16[1024,4096]{1,0:T(8,128)(2,1)} %param.5, bf16[1024,80]{0,1:T(8,128)(2,1)S(1)} %get-tuple-element.5), kind=kOutput, calls=%fused_computation | convolution fusion | flops 671088640 | bytes 9863168 | tf_op jit(solution)/shard_map/dot_general | solution.py:19
  327.5 55.9 %reduce-scatter.2.cloned.1.call-done = f32[256,80]{0,1:T(8,128)} async-done(((f32[4096,80]{0,1:T(8,128)}), f32[256,80]{0,1:T(8,128)}) %reduce-scatter.2.cloned.1.call-update) | async-done | bytes 81936 | tf_op jit(solution)/shard_map/reduce_scatter | solution.py:37
  (8 shorter events, 0.1 us)
Async XLA Ops:
  7.2 1.1 copy-start
  7.2 376.3 %reduce-scatter.2.cloned.1.call-start = ((), (), s32[]{:S(2)}) async-start(), calls=%async_computation.1 | async-start | bytes 1392640 | tf_op jit(solution)/shard_map/reduce_scatter | solution.py:37
Sparse Core Ops, SparseCore 0:
  327.7 55.7 reduce-scatter.1
where the time goes:
time: 391 us; the launch traced here: 390 us
  blocking collectives  248 us (63%)
  waiting for transfers between devices  55.9 us (14%)
  other arithmetic  44.3 us (11%)
  matrix products  26.4 us (7%)
  between operations  14.2 us (4%)
    psum x3, blocking collectives, orthonormalize(): gram_matrix = lax.psum(local_gram, 'rows')  179 us
    psum x1, blocking collectives, shards(): projection = lax.psum(transpose_product(snapshots, first_half), 'rows')  69.6 us
    reduce_scatter x1, waiting for transfers between devices, shards(): lax.psum_scatter(make_projector(snapshots, final_half), 'rows', scatter_d...  55.9 us
    another operation x9, other arithmetic, orthonormalize(): factor = jnp.linalg.cholesky(gram_matrix)  23.9 us
    another operation x6, other arithmetic, orthonormalize(): lax.linalg.triangular_solve(factor, sketch, left_side=False, lower=True,...  20.4 us
    dot_general x2, matrix products, transpose_product(): lax.dot_general(snapshots, half_basis, (((0,), (0,)), ((), ())), preferre...  11 us
  transfers between devices with their start and end apart: 1, of which 1 were waited for; matrix products, arithmetic and copies ran while one was open for 0% of the time, Pallas kernels for 0%

commit v1 on v0

v1 whole, which is shorter than its diff:
```python
import functools
import math

import jax
import jax.numpy as jnp
from jax import lax
from jax.experimental import pallas as pl
from jax.experimental.pallas import tpu as pltpu
from jax.sharding import PartitionSpec as P

MESH = pl.DeviceIdType.MESH
HIGHEST = lax.Precision.HIGHEST
BLOCK = 16
NT = (((1,), (1,)), ((), ()))
TN = (((0,), (0,)), ((), ()))


def row_digits(devices):
    digits, stride, chips = [(1, 2)], 2, devices // 2
    if (chips.bit_length() - 1) % 2:
        digits.append((stride, 2))
        stride, chips = stride * 2, chips // 2
    while chips > 1:
        digits.append((stride, 4))
        stride, chips = stride * 4, chips // 4
    return digits


def slot_of(index, digits, devices):
    slot, length = 0, devices
    for stride, size in digits:
        length //= size
        slot = slot + (index // stride) % size * length
    return slot


def inverse_factor(gram, work):
    size = gram.shape[0]
    work[pl.ds(0, size), :] = jnp.pad(gram, ((0, 0), (0, 128 - size)))
    lane = lax.broadcasted_iota(jnp.int32, (BLOCK, 128), 1)
    sub = lax.broadcasted_iota(jnp.int32, (BLOCK, 128), 0)

    def step(block, carry):
        start = pl.multiple_of(block * BLOCK, BLOCK)
        rows = work[pl.ds(start, BLOCK), :]
        rolled = pltpu.roll(rows, lax.rem(128 - start, 128), 1)
        columns = [jnp.broadcast_to(rolled[:, k:k + 1], (BLOCK, 128)) for k in range(BLOCK)]
        scale = jnp.zeros((BLOCK, 128), jnp.float32)
        for k in range(BLOCK):
            inverse = 1.0 / columns[k][k:k + 1, :]
            scale = jnp.where(sub == k, inverse, scale)
            below = sub > k
            times = jnp.where(below, columns[k] * inverse, 0.0)
            for l in range(k + 1, BLOCK):
                columns[l] = columns[l] - times * columns[l][k:k + 1, :]
            here = lane == start + k
            rows = jnp.where(here & below, 0.0, rows) - times * jnp.where(here[:1], 1.0, rows[k:k + 1, :])
            rolled = rolled - times * rolled[k:k + 1, :]
        diagonal = lane == start + sub
        unit = jnp.where(diagonal, 1.0, jnp.where((lane > start + sub) & (lane < start + BLOCK), 0.0, rows))
        update = lax.dot_general(
            rolled * scale, unit, TN, precision=HIGHEST, preferred_element_type=jnp.float32
        )
        rest = size - BLOCK
        later = pl.ds(pl.multiple_of(start + BLOCK, BLOCK), rest)
        wide = lax.broadcasted_iota(jnp.int32, (rest, 128), 1)
        old = work[later, :]
        work[later, :] = jnp.where((wide >= start) & (wide < start + BLOCK), 0.0, old) - update[BLOCK:size]
        lower = jnp.where(lane < start + sub, rows, jnp.where(diagonal, 1.0, 0.0))
        work[pl.ds(start, BLOCK), :] = lower * lax.rsqrt(1.0 / scale)
        return carry

    lax.fori_loop(0, size // BLOCK, step, 0)
    return work[pl.ds(0, size), :][:, :size]


def kernel(devices, groups_axis, rows_axis, a_hbm, tt_ref, basis_ref, coef_ref,
           a, yt, half, gram_own, gram_got, work, part, parts_got, gather, pt, cpart, cparts_got,
           a_sem, gram_sems, part_sems, gather_sems, cpart_sems):
    digits = row_digits(devices)
    me = lax.axis_index(rows_axis)
    total_rows = a.shape[0] * devices
    count, snaps = pt.shape
    rows = a.shape[0]
    width = snaps // devices
    tile = max(width, 256)
    blocks = a_sem.shape[0]
    step_rows = rows // blocks
    mine = [lax.rem(me // stride, size) for stride, size in digits]

    def peer(t, offset):
        stride, size = digits[t]
        return me + (lax.rem(mine[t] + offset, size) - mine[t]) * stride

    def copy_in(i):
        span = pl.ds(pl.multiple_of(i * step_rows, step_rows), step_rows)
        return pltpu.make_async_copy(a_hbm.at[span, :], a.at[span, :], a_sem.at[i])

    for i in range(blocks):
        copy_in(i).start()
    barrier = pltpu.get_barrier_semaphore()
    peers = 0
    for t, (stride, size) in enumerate(digits):
        for offset in range(1, size):
            pl.semaphore_signal(barrier, inc=1, device_id={rows_axis: peer(t, offset)}, device_id_type=MESH)
            peers += 1

    def send(src, dst, sems, t, offset):
        return pltpu.make_async_remote_copy(
            src_ref=src, dst_ref=dst, send_sem=sems.at[0, t, offset], recv_sem=sems.at[1, t, offset],
            device_id={rows_axis: peer(t, offset)}, device_id_type=MESH,
        )

    def gram_start(phase, t):
        copies = []
        for offset in range(1, digits[t][1]):
            copy = send(gram_own.at[phase, t], gram_got.at[phase, t, mine[t]], gram_sems.at[phase], t, offset)
            copy.start()
            copies.append(copy)
        return copies

    def gram_finish(phase, t, copies):
        for copy in copies:
            copy.wait()
        own = gram_own[phase, t]
        total = None
        for p in range(digits[t][1]):
            term = jnp.where(mine[t] == p, own, gram_got[phase, t, p])
            total = term if total is None else total + term
        if t + 1 < len(digits):
            gram_own[phase, t + 1] = total
        return total

    def local_gram(phase, matrix):
        gram_own[phase, 0] = lax.dot_general(
            matrix, matrix, NT, precision=HIGHEST, preferred_element_type=jnp.float32
        )

    def forward(i, left):
        span = pl.ds(pl.multiple_of(i * step_rows, step_rows), step_rows)
        yt[:, span] = lax.dot_general(left[...], a[span, :], NT, preferred_element_type=jnp.float32)

    def backward(target):
        def step(i, carry):
            start = pl.multiple_of(i * tile, tile)
            out = jnp.dot(half[...], a[:, pl.ds(start, tile)], preferred_element_type=jnp.float32)
            for j in range(tile // width):
                slot = slot_of(i * (tile // width) + j, digits, devices)
                target[slot] = out[:, j * width:(j + 1) * width].astype(target.dtype)
            return carry
        lax.fori_loop(0, snaps // tile, step, 0)

    def scatter_start(t, base, length, buffer, got, sems):
        copies = []
        for offset in range(1, digits[t][1]):
            p = lax.rem(mine[t] + offset, digits[t][1])
            copy = send(buffer.at[pl.ds(base + p * length, length)], got[t].at[mine[t]], sems, t, offset)
            copy.start()
            copies.append(copy)
        return copies

    def scatter_finish(t, base, length, buffer, got, copies):
        for copy in copies:
            copy.wait()
        size = digits[t][1]
        base = base + mine[t] * length

        def add(s, carry):
            total = buffer[base + s].astype(jnp.float32)
            for offset in range(1, size):
                total += got[t][lax.rem(mine[t] + offset, size), s].astype(jnp.float32)
            buffer[base + s] = total.astype(buffer.dtype)
            return carry
        lax.fori_loop(0, length, add, 0)
        return base

    def sketch(i, carry):
        copy_in(i).wait()
        forward(i, tt_ref)
        return carry

    lax.fori_loop(0, blocks, sketch, 0)
    local_gram(0, yt[...])
    pl.semaphore_wait(barrier, peers)
    for t in range(len(digits)):
        gram = gram_finish(0, t, gram_start(0, t))
    inverse = inverse_factor(gram, work)
    half[...] = jnp.dot(inverse, yt[...], precision=HIGHEST, preferred_element_type=jnp.float32).astype(half.dtype)

    backward(part)
    base, length, bases = 0, devices, []
    for t, (stride, size) in enumerate(digits):
        length //= size
        bases.append(base)
        base = scatter_finish(t, base, length, part, parts_got,
                              scatter_start(t, base, length, part, parts_got, part_sems))
    gather[base] = part[base].astype(gather.dtype)
    length = 1
    for t in reversed(range(len(digits))):
        copies = []
        for offset in range(1, digits[t][1]):
            span = gather.at[pl.ds(base, length)]
            copy = send(span, span, gather_sems, t, offset)
            copy.start()
            copies.append(copy)
        for copy in copies:
            copy.wait()
        base = bases[t]
        length *= digits[t][1]
    for d in range(devices):
        pt[:, d * width:(d + 1) * width] = gather[slot_of(d, digits, devices)]

    def power(i, carry):
        forward(i, pt)
        return carry

    lax.fori_loop(0, blocks, power, 0)
    local_gram(1, yt[...])
    for t in range(len(digits)):
        gram = gram_finish(1, t, gram_start(1, t))
    inverse = inverse_factor(gram, work)
    first = jnp.dot(inverse, yt[...], precision=HIGHEST, preferred_element_type=jnp.float32)
    yt[...] = first
    half[...] = first.astype(half.dtype)
    local_gram(2, first)
    gram_copies = gram_start(2, 0)
    backward(cpart)
    base, length = 0, devices
    for t, (stride, size) in enumerate(digits):
        length //= size
        copies = scatter_start(t, base, length, cpart, cparts_got, cpart_sems)
        gram = gram_finish(2, t, gram_copies)
        if t + 1 < len(digits):
            gram_copies = gram_start(2, t + 1)
        else:
            inverse = inverse_factor(gram, work)
            last = jnp.dot(inverse, yt[...], precision=HIGHEST, preferred_element_type=jnp.float32)
            basis_ref[...] = (last * math.sqrt(total_rows)).T
        base = scatter_finish(t, base, length, cpart, cparts_got, copies)
    coef = jnp.dot(inverse, cpart[base].astype(jnp.float32), precision=HIGHEST, preferred_element_type=jnp.float32)
    coef_ref[...] = coef.T


def shards(snapshots, test_matrix):
    devices = lax.axis_size("rows")
    rows, snaps = snapshots.shape
    count = test_matrix.shape[1]
    digits = row_digits(devices)
    width = snaps // devices
    stages = len(digits)
    widest = max(size for _, size in digits)
    blocks = 8
    got, length = [], devices
    for _, size in digits:
        length //= size
        got.append((size, length, count, width))
    f32, bf16 = jnp.float32, jnp.bfloat16
    vmem = pl.BlockSpec(memory_space=pltpu.VMEM)
    return pl.pallas_call(
        functools.partial(kernel, devices, "groups", "rows"),
        out_shape=(
            jax.ShapeDtypeStruct((rows, count), f32),
            jax.ShapeDtypeStruct((width, count), f32),
        ),
        in_specs=[pl.BlockSpec(memory_space=pl.ANY), vmem],
        out_specs=(vmem, vmem),
        scratch_shapes=[
            pltpu.VMEM((rows, snaps), bf16),
            pltpu.VMEM((count, rows), f32),
            pltpu.VMEM((count, rows), bf16),
            pltpu.VMEM((3, stages, count, count), f32),
            pltpu.VMEM((3, stages, widest, count, count), f32),
            pltpu.VMEM((2 * count, 128), f32),
            pltpu.VMEM((devices, count, width), f32),
            [pltpu.VMEM(shape, f32) for shape in got],
            pltpu.VMEM((devices, count, width), bf16),
            pltpu.VMEM((count, snaps), bf16),
            pltpu.VMEM((devices, count, width), bf16),
            [pltpu.VMEM(shape, bf16) for shape in got],
            pltpu.SemaphoreType.DMA((blocks,)),
            pltpu.SemaphoreType.DMA((3, 2, stages, widest)),
            pltpu.SemaphoreType.DMA((2, stages, widest)),
            pltpu.SemaphoreType.DMA((2, stages, widest)),
            pltpu.SemaphoreType.DMA((2, stages, widest)),
        ],
        compiler_params=pltpu.CompilerParams(
            collective_id=0, has_side_effects=True, vmem_limit_bytes=56 * 2**20
        ),
    )(snapshots, test_matrix.T)


def solution(mesh):
    in_specs = (P(("groups", "rows"), None), P())
    out_specs = (P(("groups", "rows"), None), P(("groups", "rows"), None))
    return jax.shard_map(shards, mesh=mesh, in_specs=in_specs, out_specs=out_specs, check_vma=False)
```

time: 391 us -> 95.5 us (0.24)
  blocking collectives: 248 us -> 0 us
  Pallas kernels: 0 us -> 91.1 us
  waiting for transfers between devices: 55.9 us -> 0 us
  other arithmetic: 44.3 us -> 0 us
  matrix products: 26.4 us -> 0 us
  between operations: 14.2 us -> 0.64 us
    psum x4 -> x0, blocking collectives: 248 us -> none  [the longest x3 179 us: orthonormalize(): gram_matrix = lax.psum(local_gram, 'rows')]
    pallas_call x0 -> x1, Pallas kernels: none -> 91.1 us  [shards(): pl.pallas_call(functools.partial(kernel, devices, 'groups', 'rows'), out_...]
    reduce_scatter x1 -> x0, waiting for transfers between devices: 55.9 us -> none  [shards(): lax.psum_scatter(make_projector(snapshots, final_half), 'rows', scatter_d...]
    another operation x15 -> x0, other arithmetic: 44.3 us -> none  [the longest x9 23.9 us: orthonormalize(): factor = jnp.linalg.cholesky(gram_matrix)]
    dot_general x7 -> x0, matrix products: 24.3 us -> none  [the longest x2 11 us: transpose_product(): lax.dot_general(snapshots, half_basis, (((0,), (0,)), ((), ())), preferre...]
  transfers between devices with their start and end apart: 1 -> 0, of which waited for: 1 -> 0; matrix products, arithmetic and copies ran while one was open for 0% -> 0% of each run, Pallas kernels for 0% -> 0%
where the time goes in v1:
time: 95.5 us; the launch traced here: 95.3 us
  Pallas kernels  91.1 us (95%)
  local copies, waits for them, and re-layouts  3.58 us (4%)
    pallas_call x1, Pallas kernels, shards(): pl.pallas_call(functools.partial(kernel, devices, 'groups', 'rows'), out_...  91.1 us
    pallas_call x2, local copies, waits for them, and re-layouts, shards(): pl.pallas_call(functools.partial(kernel, devices, 'groups', 'rows'), out_...  3.58 us

profile of v1, /device:TPU:0, one launch (start us, length us, event | category | flops | bytes accessed | tf_op | source)
XLA Modules:
  0.0 95.3 jit_solution(5665911847885586548)
XLA Ops:
  0.6 91.1 %shard_map.41 = (f32[1024,80]{1,0:T(8,128)}, f32[256,80]{1,0:T(8,128)}) custom-call(bf16[1024,4096]{1,0:T(8,128)(2,1)} %a_hbm.1, bf16[80,4096]{1,0:T(8,128)(2,1)} %bitcast.1), custom_call_target="tpu_custom_call" | custom-call | tf_op jit(solution)/shard_map/pallas_call | solution.py:259
  91.7 2.0 %copy.4 = f32[1024,80]{0,1:T(8,128)} copy(f32[1024,80]{1,0:T(8,128)} %get-tuple-element.2) | data formatting | bytes 655360 | tf_op jit(solution)/shard_map/pallas_call | solution.py:259
  93.6 1.6 %copy.5 = f32[256,80]{0,1:T(8,128)} copy(f32[256,80]{1,0:T(8,128)} %get-tuple-element.3) | data formatting | bytes 163840 | tf_op jit(solution)/shard_map/pallas_call | solution.py:259

commit v2 on v1

--- a/solution.py
+++ b/solution.py
@@ -1,4 +1,5 @@
 import functools
+import itertools
 import math
 
 import jax
@@ -26,17 +27,35 @@
     return digits
 
 
-def slot_of(index, digits, devices):
-    slot, length = 0, devices
-    for stride, size in digits:
-        length //= size
-        slot = slot + (index // stride) % size * length
-    return slot
-
-
-def inverse_factor(gram, work):
+def offsets_of(digits):
+    offsets = list(itertools.product(*[range(size) for _, size in digits]))
+    return sorted(offsets, key=lambda o: [o[t] == 0 for t in range(len(o))])
+
+
+def number_of(offset, digits, first=0):
+    number = 0
+    for t in range(first, len(digits)):
+        number = number * digits[t][1] + offset[t]
+    return number
+
+
+def split_of(size):
+    return -(-size // (2 * BLOCK)) * BLOCK
+
+
+def packed(gram):
     size = gram.shape[0]
-    work[pl.ds(0, size), :] = jnp.pad(gram, ((0, 0), (0, 128 - size)))
+    split = split_of(size)
+    wide = jnp.pad(gram, ((0, 0), (0, 128 - size)))
+    beside = jnp.pad(pltpu.roll(wide[split:], size - split, 1), ((0, 2 * split - size), (0, 0)))
+    lane = lax.broadcasted_iota(jnp.int32, (split, 128), 1)
+    return jnp.where(lane < size, wide[:split], jnp.where(lane < 2 * size - split, beside, 0.0))
+
+
+def inverse_factor(gram, work, size):
+    split, rest = gram.shape[0], size - gram.shape[0]
+    work[pl.ds(0, split), :] = gram
+    work[pl.ds(split, rest), :] = pltpu.roll(gram[:rest], 128 - (size - split), 1)
     lane = lax.broadcasted_iota(jnp.int32, (BLOCK, 128), 1)
     sub = lax.broadcasted_iota(jnp.int32, (BLOCK, 128), 0)
 
@@ -132,47 +151,113 @@
         return total
 
     def local_gram(phase, matrix):
-        gram_own[phase, 0] = lax.dot_general(
+        gram_own[phase, 0] = packed(lax.dot_general(
             matrix, matrix, NT, precision=HIGHEST, preferred_element_type=jnp.float32
-        )
+        ))
 
     def forward(i, left):
         span = pl.ds(pl.multiple_of(i * step_rows, step_rows), step_rows)
         yt[:, span] = lax.dot_general(left[...], a[span, :], NT, preferred_element_type=jnp.float32)
 
-    def backward(target):
-        def step(i, carry):
-            start = pl.multiple_of(i * tile, tile)
-            out = jnp.dot(half[...], a[:, pl.ds(start, tile)], preferred_element_type=jnp.float32)
-            for j in range(tile // width):
-                slot = slot_of(i * (tile // width) + j, digits, devices)
-                target[slot] = out[:, j * width:(j + 1) * width].astype(target.dtype)
-            return carry
-        lax.fori_loop(0, snaps // tile, step, 0)
-
-    def scatter_start(t, base, length, buffer, got, sems):
-        copies = []
-        for offset in range(1, digits[t][1]):
-            p = lax.rem(mine[t] + offset, digits[t][1])
-            copy = send(buffer.at[pl.ds(base + p * length, length)], got[t].at[mine[t]], sems, t, offset)
+    def moved(offset, sign):
+        place = me
+        for t, (stride, size) in enumerate(digits):
+            if offset[t]:
+                place = place + (lax.rem(mine[t] + sign * offset[t] + size, size) - mine[t]) * stride
+        return place
+
+    def change(offset, t, value):
+        return offset[:t] + (value,) + offset[t + 1:]
+
+    aligned = width % 128 == 0
+
+    def columns_of(place):
+        return pl.ds(pl.multiple_of(place * width, width), width)
+
+    def scatter(buffer, got, sems):
+        copies = {}
+
+        def compute(offset):
+            if aligned:
+                place = moved(offset, 1)
+                out = jnp.dot(half[...], a[:, columns_of(place)], preferred_element_type=jnp.float32)
+                buffer[place] = out.astype(buffer.dtype)
+
+        def put(t, offset):
+            copies[offset] = copy = pltpu.make_async_remote_copy(
+                src_ref=buffer.at[moved(offset, 1)],
+                dst_ref=got[t].at[offset[t] - 1, number_of(offset, digits, t + 1)],
+                send_sem=sems.at[0, number_of(offset, digits)], recv_sem=sems.at[1, number_of(offset, digits)],
+                device_id={rows_axis: peer(t, offset[t])}, device_id_type=MESH,
+            )
             copy.start()
-            copies.append(copy)
-        return copies
-
-    def scatter_finish(t, base, length, buffer, got, copies):
-        for copy in copies:
-            copy.wait()
-        size = digits[t][1]
-        base = base + mine[t] * length
-
-        def add(s, carry):
-            total = buffer[base + s].astype(jnp.float32)
-            for offset in range(1, size):
-                total += got[t][lax.rem(mine[t] + offset, size), s].astype(jnp.float32)
-            buffer[base + s] = total.astype(buffer.dtype)
-            return carry
-        lax.fori_loop(0, length, add, 0)
-        return base
+
+        def take(t, offset):
+            place = moved(offset, 1)
+            total = buffer[place].astype(jnp.float32)
+            for p in range(1, digits[t][1]):
+                copies[change(offset, t, p)].wait_recv()
+                total += got[t][p - 1, number_of(offset, digits, t + 1)].astype(jnp.float32)
+            buffer[place] = total.astype(buffer.dtype)
+            if t + 1 < len(digits) and offset[t + 1]:
+                put(t + 1, offset)
+
+        if not aligned:
+            def step(i, carry):
+                start = pl.multiple_of(i * tile, tile)
+                out = jnp.dot(half[...], a[:, pl.ds(start, tile)], preferred_element_type=jnp.float32)
+                for j in range(tile // width):
+                    buffer[i * (tile // width) + j] = out[:, j * width:(j + 1) * width].astype(buffer.dtype)
+                return carry
+            lax.fori_loop(0, snaps // tile, step, 0)
+        held = [o for o in offsets_of(digits) if o[0] == 0]
+        for i, offset in enumerate(held):
+            for p in range(1, digits[0][1]):
+                compute(change(offset, 0, p))
+                put(0, change(offset, 0, p))
+            compute(offset)
+            if i >= 2:
+                take(0, held[i - 2])
+            yield
+        for offset in held[-2:]:
+            take(0, offset)
+            yield
+        for t in range(1, len(digits)):
+            for offset in held:
+                if not any(offset[:t + 1]):
+                    take(t, offset)
+                    yield
+        for copy in copies.values():
+            copy.wait_send()
+
+    def spread(use):
+        copies = {}
+
+        def forward_to(t, offset):
+            block = gather.at[moved(offset, -1)]
+            for p in range(1, digits[t][1]):
+                there = change(offset, t, p)
+                number = number_of(there, digits)
+                copies[there] = copy = pltpu.make_async_remote_copy(
+                    src_ref=block, dst_ref=block, send_sem=gather_sems.at[0, number],
+                    recv_sem=gather_sems.at[1, number],
+                    device_id={rows_axis: peer(t, p)}, device_id_type=MESH,
+                )
+                copy.start()
+
+        def arrived(last, offset):
+            for t in reversed(range(last)):
+                forward_to(t, offset)
+            use(moved(offset, -1), not any(offset))
+
+        arrived(len(digits), (0,) * len(digits))
+        for t in reversed(range(len(digits))):
+            for offset in reversed(offsets_of(digits)):
+                if offset[t] and not any(offset[:t]):
+                    copies[offset].wait_recv()
+                    arrived(t, offset)
+        for copy in copies.values():
+            copy.wait_send()
 
     def sketch(i, carry):
         copy_in(i).wait()
@@ -184,61 +269,51 @@
     pl.semaphore_wait(barrier, peers)
     for t in range(len(digits)):
         gram = gram_finish(0, t, gram_start(0, t))
-    inverse = inverse_factor(gram, work)
+    inverse = inverse_factor(gram, work, count)
     half[...] = jnp.dot(inverse, yt[...], precision=HIGHEST, preferred_element_type=jnp.float32).astype(half.dtype)
 
-    backward(part)
-    base, length, bases = 0, devices, []
-    for t, (stride, size) in enumerate(digits):
-        length //= size
-        bases.append(base)
-        base = scatter_finish(t, base, length, part, parts_got,
-                              scatter_start(t, base, length, part, parts_got, part_sems))
-    gather[base] = part[base].astype(gather.dtype)
-    length = 1
-    for t in reversed(range(len(digits))):
-        copies = []
-        for offset in range(1, digits[t][1]):
-            span = gather.at[pl.ds(base, length)]
-            copy = send(span, span, gather_sems, t, offset)
-            copy.start()
-            copies.append(copy)
-        for copy in copies:
-            copy.wait()
-        base = bases[t]
-        length *= digits[t][1]
-    for d in range(devices):
-        pt[:, d * width:(d + 1) * width] = gather[slot_of(d, digits, devices)]
-
-    def power(i, carry):
-        forward(i, pt)
-        return carry
-
-    lax.fori_loop(0, blocks, power, 0)
+    for _ in scatter(part, parts_got, part_sems):
+        pass
+    gather[me] = part[me].astype(gather.dtype)
+
+    def power(place, is_first):
+        if aligned:
+            term = lax.dot_general(gather[place], a[:, columns_of(place)], NT, preferred_element_type=jnp.float32)
+            yt[...] = term if is_first else yt[...] + term
+
+    spread(power)
+    if not aligned:
+        for d in range(devices):
+            pt[:, d * width:(d + 1) * width] = gather[d]
+
+        def power_rows(i, carry):
+            forward(i, pt)
+            return carry
+
+        lax.fori_loop(0, blocks, power_rows, 0)
     local_gram(1, yt[...])
     for t in range(len(digits)):
         gram = gram_finish(1, t, gram_start(1, t))
-    inverse = inverse_factor(gram, work)
+    inverse = inverse_factor(gram, work, count)
     first = jnp.dot(inverse, yt[...], precision=HIGHEST, preferred_element_type=jnp.float32)
     yt[...] = first
     half[...] = first.astype(half.dtype)
     local_gram(2, first)
-    gram_copies = gram_start(2, 0)
-    backward(cpart)
-    base, length = 0, devices
-    for t, (stride, size) in enumerate(digits):
-        length //= size
-        copies = scatter_start(t, base, length, cpart, cparts_got, cpart_sems)
+    steps = scatter(cpart, cparts_got, cpart_sems)
+    held = devices // digits[0][1]
+    for t in range(len(digits)):
+        gram_copies = gram_start(2, t)
+        for _ in range(held // len(digits) + 1):
+            next(steps, None)
         gram = gram_finish(2, t, gram_copies)
-        if t + 1 < len(digits):
-            gram_copies = gram_start(2, t + 1)
-        else:
-            inverse = inverse_factor(gram, work)
-            last = jnp.dot(inverse, yt[...], precision=HIGHEST, preferred_element_type=jnp.float32)
-            basis_ref[...] = (last * math.sqrt(total_rows)).T
-        base = scatter_finish(t, base, length, cpart, cparts_got, copies)
-    coef = jnp.dot(inverse, cpart[base].astype(jnp.float32), precision=HIGHEST, preferred_element_type=jnp.float32)
-    coef_ref[...] = coef.T
+    inverse = inverse_factor(gram, work, count)
+    last = jnp.dot(inverse, yt[...], precision=HIGHEST, preferred_element_type=jnp.float32)
+    basis_ref[...] = last * math.sqrt(total_rows)
+    for _ in steps:
+        pass
+    coef_ref[...] = jnp.dot(
+        inverse, cpart[me].astype(jnp.float32), precision=HIGHEST, preferred_element_type=jnp.float32
+    )
 
 
 def shards(snapshots, test_matrix):
@@ -253,14 +328,14 @@
     got, length = [], devices
     for _, size in digits:
         length //= size
-        got.append((size, length, count, width))
+        got.append((size - 1, length, count, width))
     f32, bf16 = jnp.float32, jnp.bfloat16
     vmem = pl.BlockSpec(memory_space=pltpu.VMEM)
-    return pl.pallas_call(
+    basis, coefficients = pl.pallas_call(
         functools.partial(kernel, devices, "groups", "rows"),
         out_shape=(
-            jax.ShapeDtypeStruct((rows, count), f32),
-            jax.ShapeDtypeStruct((width, count), f32),
+            jax.ShapeDtypeStruct((count, rows), f32),
+            jax.ShapeDtypeStruct((count, width), f32),
         ),
         in_specs=[pl.BlockSpec(memory_space=pl.ANY), vmem],
         out_specs=(vmem, vmem),
@@ -268,8 +343,8 @@
             pltpu.VMEM((rows, snaps), bf16),
             pltpu.VMEM((count, rows), f32),
             pltpu.VMEM((count, rows), bf16),
-            pltpu.VMEM((3, stages, count, count), f32),
-            pltpu.VMEM((3, stages, widest, count, count), f32),
+            pltpu.VMEM((3, stages, split_of(count), 128), f32),
+            pltpu.VMEM((3, stages, widest, split_of(count), 128), f32),
             pltpu.VMEM((2 * count, 128), f32),
             pltpu.VMEM((devices, count, width), f32),
             [pltpu.VMEM(shape, f32) for shape in got],
@@ -279,14 +354,15 @@
             [pltpu.VMEM(shape, bf16) for shape in got],
             pltpu.SemaphoreType.DMA((blocks,)),
             pltpu.SemaphoreType.DMA((3, 2, stages, widest)),
-            pltpu.SemaphoreType.DMA((2, stages, widest)),
-            pltpu.SemaphoreType.DMA((2, stages, widest)),
-            pltpu.SemaphoreType.DMA((2, stages, widest)),
+            pltpu.SemaphoreType.DMA((2, devices)),
+            pltpu.SemaphoreType.DMA((2, devices)),
+            pltpu.SemaphoreType.DMA((2, devices)),
         ],
         compiler_params=pltpu.CompilerParams(
             collective_id=0, has_side_effects=True, vmem_limit_bytes=56 * 2**20
         ),
     )(snapshots, test_matrix.T)
+    return basis.T, coefficients.T
 
 
 def solution(mesh):

time: 95.5 us -> 82.1 us (0.86)
  Pallas kernels: 91.1 us -> 78 us
    pallas_call x1, Pallas kernels: 91.1 us -> 78 us  [shards(): pl.pallas_call(functools.partial(kernel, devices, 'groups', 'rows'), out_...]
    pallas_call x2 -> x0, local copies, waits for them, and re-layouts: 3.58 us -> none  [shards(): pl.pallas_call(functools.partial(kernel, devices, 'groups', 'rows'), out_...]
    unnamed x0 -> x2, local copies, waits for them, and re-layouts: none -> 3.25 us
where the time goes in v2:
time: 82.1 us; the launch traced here: 81.9 us
  Pallas kernels  78 us (95%)
  local copies, waits for them, and re-layouts  3.25 us (4%)
    pallas_call x1, Pallas kernels, shards(): pl.pallas_call(functools.partial(kernel, devices, 'groups', 'rows'), out_...  78 us
    unnamed x2, local copies, waits for them, and re-layouts  3.25 us

profile of v2, /device:TPU:0, one launch (start us, length us, event | category | flops | bytes accessed | tf_op | source)
XLA Modules:
  0.0 81.9 jit_solution(9713613463179713529)
XLA Ops:
  0.6 78.0 %shard_map.41 = (f32[80,1024]{1,0:T(8,128)}, f32[80,256]{1,0:T(8,128)}) custom-call(bf16[1024,4096]{1,0:T(8,128)(2,1)} %a_hbm.1, bf16[80,4096]{1,0:T(8,128)(2,1)} %bitcast.3), custom_call_target="tpu_custom_call" | custom-call | tf_op jit(solution)/shard_map/pallas_call | solution.py:334
  78.6 1.7 %copy.6 = f32[1024,80]{0,1:T(8,128)} copy(f32[1024,80]{0,1:T(8,128)} %bitcast.4) | data formatting | bytes 655360
  80.4 1.5 %copy.7 = f32[256,80]{0,1:T(8,128)} copy(f32[256,80]{0,1:T(8,128)} %bitcast.5) | data formatting | bytes 163840
